TPU v7x, 32 devices: a whole 2x2x4 slice. The times are simulated.
32 devices in a mesh: fsdp: 8 (over z, x), rep: 4 (over y, core).
Axes of the slice: x: 2, y: 2, z: 4, core: 2. Of those that a mesh axis runs over, the one named last changes fastest.
Arguments:
- gate_shards: bfloat16 [4, 7168, 2048], P(None, 'fsdp', 'rep'), may hold values from -6 to 6
- up_shards: bfloat16 [4, 7168, 2048], P(None, 'fsdp', 'rep'), may hold values from -6 to 6
- norm_gain: float32 [7168], P('fsdp'), may hold values from 0.1 to 1.9
- matching: int32 [8], replicated, may hold values from 0 to 7, each once
- replica_slots: int32 [4, 4], replicated, may hold values from 0 to 7, as said below
- replica_count: int32 [4], replicated, may hold values from 1 to 4, as said below
Outputs:
- joined: bfloat16 [8, 7168, 4096], P('fsdp')
Inputs may be any that keep to these rules, and one draw needn't show every extreme that they name: `replica_slots`: every physical slot 0 to 7 appears exactly once among the first replica_count[e] entries of the rows e together; those entries of a row are ascending; the remaining entries of a row are arbitrary slots. `replica_count`: the counts sum to 8 and stay at or below 4; one expert has exactly 4 replicas in every draw. `matching`: each rank appears once.
All inputs are finite; a program needn't handle non-finite values.
Results may differ from a plain program's by a relative error of at most 0.001.
Values may be sent and summed in bfloat16 or wider, within the bound.
A program may use at most 256 MiB of HBM per device.

v0:
```python
import jax
import jax.numpy as jnp
from jax import lax
from jax.sharding import PartitionSpec as P


def slot_owner(replica_slots, replica_count, slots):
    live = jnp.arange(replica_slots.shape[1])[None, :] < replica_count[:, None]
    hits = live[:, :, None] & (replica_slots[:, :, None] == jnp.arange(slots)[None, None, :])
    owners = jnp.arange(replica_slots.shape[0], dtype=jnp.int32)[:, None, None] * hits.astype(
        jnp.int32
    )
    return jnp.sum(owners, axis=(0, 1))


def inverse_order(matching):
    count = matching.shape[0]
    match_grid = matching[None, :] == jnp.arange(count, dtype=jnp.int32)[:, None]
    ranks = jnp.where(match_grid, jnp.arange(count, dtype=jnp.int32)[None, :], 0)
    return jnp.sum(ranks, axis=1)


def fold_rows(weights, gain_rows):
    return (weights.astype(jnp.float32) * gain_rows[:, None]).astype(jnp.bfloat16)


def pick_units(weights, expert_pick, block_pick, block_count):
    experts, rows, units = weights.shape
    return weights.reshape(experts, rows, units // block_count, block_count)[
        expert_pick, :, :, block_pick
    ]


def alternate(gate_part, up_part):
    shape = gate_part.shape
    return jnp.stack((gate_part, up_part), axis=-1).reshape(shape[:-1] + (2 * shape[-1],))


def local(gate_shards, up_shards, norm_gain, matching, replica_slots, replica_count):
    devices = lax.axis_size("fsdp")
    block_count = min(8, devices // 8)
    rows = gate_shards.shape[1]
    owners = slot_owner(replica_slots, replica_count, devices // block_count)
    targets = jnp.arange(devices, dtype=jnp.int32)
    expert_pick = owners[targets // block_count]
    block_pick = targets % block_count
    inverse = inverse_order(matching)
    gate_all, up_all = (
        lax.all_gather(gate_shards, "rep", axis=2, tiled=True),
        lax.all_gather(up_shards, "rep", axis=2, tiled=True),
    )
    outgoing = alternate(
        pick_units(gate_all, expert_pick, block_pick, block_count),
        pick_units(up_all, expert_pick, block_pick, block_count),
    )
    received = lax.all_to_all(outgoing, "fsdp", split_axis=0, concat_axis=0, tiled=True)
    portion = received[inverse].reshape(devices * rows, received.shape[2])
    gain_all = lax.all_gather(norm_gain, "fsdp", axis=0, tiled=True)
    gain_model = gain_all.reshape(devices, rows)[inverse].reshape(devices * rows)
    portion = fold_rows(portion, gain_model)
    return portion[None]


def solution(mesh):
    return jax.shard_map(
        local,
        mesh=mesh,
        in_specs=(P(None, "fsdp", "rep"), P(None, "fsdp", "rep"), P("fsdp"), P(), P(), P()),
        out_specs=P("fsdp", None, None),
        check_vma=False,
    )
```

profile of v0, /device:TPU:9, one launch (start us, length us, event | category | flops | bytes accessed | tf_op | source)
XLA Modules:
  0.0 1923.1 jit_solution(4853650690791676788)
XLA Ops:
  6.5 0.0 all-gather.4.cloned.1.call-start
  6.5 0.7 all-gather.4.cloned.1.call-update
  7.3 0.0 all-gather.6.cloned.1.call-start
  7.3 0.7 all-gather.6.cloned.1.call-update
  8.0 0.7 iota_compare_fusion.2
  8.8 0.8 select_reduce_fusion
  9.5 0.6 gather_fusion
  10.2 94.4 %all-gather.4.cloned.1.call-done = bf16[4,896,2048]{2,1,0:T(8,128)(2,1)} async-done(((bf16[4,896,512]{2,1,0:T(8,128)(2,1)}), bf16[4,896,2048]{2,1,0:T(8,128)(2,1)}) %all-gather.4.cloned.1.call-update) | async-done | bytes 14680080 | tf_op jit(solution)/shard_map/all_gather | solution.py:49
  104.6 11.3 fusion.7
  115.9 11.5 gather_fusion.2
  127.4 10.6 gather_fusion.3
  138.0 62.2 %all-gather.6.cloned.1.call-done = bf16[4,896,2048]{2,1,0:T(8,128)(2,1)} async-done(((bf16[4,896,512]{2,1,0:T(8,128)(2,1)}), bf16[4,896,2048]{2,1,0:T(8,128)(2,1)}) %all-gather.6.cloned.1.call-update) | async-done | bytes 14680080 | tf_op jit(solution)/shard_map/all_gather | solution.py:50
  200.2 10.5 fusion.8
  210.7 10.2 gather_fusion.4
  220.9 10.2 gather_fusion.5
  231.1 38.8 %maximum_bitcast_fusion = (bf16[8,896,2048,1]{2,1,0,3:T(8,128)(2,1)}, bf16[8,896,2048,1]{2,1,0,3:T(8,128)(2,1)}) fusion(bf16[8,896,1024]{2,1,0:T(8,128)(2,1)} %gather_fusion.3, bf16[8,896,1024]{2,1,0:T(8,128)(2,1)} %gather_fusion.2, bf16[8,896,1024]{2,1,0:T(8,128)(2,1)} %gather_fusion.5, bf16[8,896,1024]{2,1,0:T(8,128)(2,1)} %gather_fusion.4), kind=kLoop, calls=%fused_computation.14 | loop fusion | flops 117440512 | bytes 117440512 | tf_op jit(solution)/shard_map/stack | solution.py:36
  269.9 39.1 %pad_maximum_fusion = bf16[8,896,2048,2]{2,1,0,3:T(8,128)(2,1)} fusion(bf16[8,896,2048,1]{2,1,0,3:T(8,128)(2,1)} %get-tuple-element.14, bf16[8,896,2048,1]{2,1,0,3:T(8,128)(2,1)} %get-tuple-element.13), kind=kLoop, calls=%fused_computation.12 | loop fusion | flops 29360128 | bytes 117440512 | tf_op jit(solution)/shard_map/stack | solution.py:36
  308.9 80.1 %copy.12 = bf16[8,896,2048,2]{1,0,3,2:T(8,128)(2,1)} copy(bf16[8,896,2048,2]{2,1,0,3:T(8,128)(2,1)} %pad_maximum_fusion) | data formatting | bytes 117440512 | tf_op jit(solution)/shard_map/stack | solution.py:36
  389.1 74.2 %copy.13 = bf16[8,896,4096]{2,1,0:T(8,128)(2,1)} copy(bf16[8,896,4096]{1,0,2:T(8,128)(2,1)} %bitcast.23) | data formatting | bytes 117440512 | tf_op jit(solution)/shard_map/reshape | solution.py:36
  463.3 0.0 copy-start
  463.3 0.0 copy-start.1
  463.3 9.5 all-to-all-start
  472.8 0.0 copy-done
  472.8 1273.6 %all-gather = f32[8,1,896]{2,1,0:T(1,128)S(1)} all-gather(f32[1,1,896]{2,1,0:T(1,128)S(1)} %reshape.187), channel_id=1, replica_groups=mesh['fsdp'=8,'rep'=4] {'fsdp'}, dimensions={0}, use_global_device_ids=true | all-gather | bytes 32256 | tf_op jit(solution)/shard_map/all_gather | solution.py:58
  1746.4 0.0 copy-done.1
  1746.4 0.1 select_reduce_fusion.1
  1746.5 0.6 gather_fusion.1
  1747.1 0.0 all-to-all-done
  1747.1 41.2 %fusion.6 = (bf16[8,896,1024]{2,1,0:T(8,128)(2,1)}, bf16[8,896,1024]{2,1,0:T(8,128)(2,1)}, bf16[8,896,1024]{2,1,0:T(8,128)(2,1)}, bf16[8,896,1024]{2,1,0:T(8,128)(2,1)}) fusion(bf16[8,896,4096]{2,1,0:T(8,128)(2,1)} %all-to-all-done), kind=kLoop, calls=%fused_computation.31 | loop fusion | bytes 117440512 | tf_op jit(solution)/shard_map/gather | solution.py:57
  1788.4 12.4 gather_fusion.6
  1800.7 12.4 gather_fusion.7
  1813.2 12.5 gather_fusion.8
  1825.6 12.3 gather_fusion.9
  1838.0 39.0 %pad_maximum_fusion.1 = bf16[8,896,4096]{2,1,0:T(8,128)(2,1)} fusion(bf16[8,896,1024]{2,1,0:T(8,128)(2,1)} %gather_fusion.9, bf16[8,896,1024]{2,1,0:T(8,128)(2,1)} %gather_fusion.8, bf16[8,896,1024]{2,1,0:T(8,128)(2,1)} %gather_fusion.7, bf16[8,896,1024]{2,1,0:T(8,128)(2,1)} %gather_fusion.6), kind=kLoop, calls=%fused_computation.13 | loop fusion | flops 234881024 | bytes 117440512
  1876.9 39.3 %fusion = bf16[1,7168,4096]{2,1,0:T(8,128)(2,1)} fusion(f32[7168]{0:T(1024)S(1)} %mul.27, bf16[1,7168,4096]{2,1,0:T(8,128)(2,1)} %bitcast.22), kind=kLoop, calls=%fused_computation.11 | loop fusion | flops 88080384 | bytes 117469184 | tf_op jit(solution)/shard_map/convert_element_type | solution.py:24
  (8 shorter events, 0.0 us)
Async XLA Ops:
  6.5 98.0 %all-gather.4.cloned.1.call-start = ((), (), s32[]{:S(2)}) async-start(), calls=%async_computation.1 | async-start | bytes 18350080 | tf_op jit(solution)/shard_map/all_gather | solution.py:49
  7.3 192.9 %all-gather.6.cloned.1.call-start = ((), (), s32[]{:S(2)}) async-start(), calls=%async_computation.2 | async-start | bytes 18350080 | tf_op jit(solution)/shard_map/all_gather | solution.py:50
  463.3 9.5 copy-start
  463.3 1283.1 %copy-start.1 = (s32[8]{0:T(128)S(1)}, s32[8]{0:T(128)}, u32[]{:S(2)}) copy-start(s32[8]{0:T(128)} %param.9) | copy-start | bytes 100
  463.3 1283.8 %all-to-all-start = ((bf16[8,896,4096]{2,1,0:T(8,128)(2,1)}), bf16[8,896,4096]{2,1,0:T(8,128)(2,1)}, u32[]{:S(2)}, u32[]{:S(2)}) async-start(bf16[8,896,4096]{2,1,0:T(8,128)(2,1)} %copy.13), calls=%async_computation | async-start | bytes 117440512 | tf_op jit(solution)/shard_map/all_to_all | solution.py:56
Sparse Core Ops, SparseCore 0:
  8.9 95.5 all-gather.3
  106.1 94.0 all-gather.5
where the time goes:
time: 1940 us; the launch traced here: 1920 us
  blocking collectives  1270 us (65%)
  local copies, waits for them, and re-layouts  311 us (16%)
  waiting for transfers between devices  158 us (8%)
  other arithmetic  158 us (8%)
    all_gather x1, blocking collectives, local(): gain_all = lax.all_gather(norm_gain, 'fsdp', axis=0, tiled=True)  1270 us
    all_gather x1, waiting for transfers between devices, local(): lax.all_gather(gate_shards, 'rep', axis=2, tiled=True)  94.4 us
    gather x5, local copies, waits for them, and re-layouts, local(): portion = received[inverse].reshape(devices * rows, received.shape[2])  90.8 us
    another operation x1, local copies, waits for them, and re-layouts, alternate(): jnp.stack((gate_part, up_part), axis=-1)  80.1 us
    another operation x2, other arithmetic, alternate(): jnp.stack((gate_part, up_part), axis=-1)  77.8 us
    reshape x1, local copies, waits for them, and re-layouts, alternate(): jnp.stack((gate_part, up_part), axis=-1)  74.2 us
    gather x6, local copies, waits for them, and re-layouts, pick_units(): weights.reshape(experts, rows, units // block_count, block_count)  64.4 us
    all_gather x1, waiting for transfers between devices, local(): lax.all_gather(up_shards, 'rep', axis=2, tiled=True)  62.2 us
  transfers between devices with their start and end apart: 3, of which 2 were waited for; matrix products, arithmetic and copies ran while one was open for 2% of the time, Pallas kernels for 0%

commit v1 on v0

--- a/solution.py
+++ b/solution.py
@@ -1,6 +1,10 @@
+import functools
+
 import jax
 import jax.numpy as jnp
 from jax import lax
+from jax.experimental import pallas as pl
+from jax.experimental.pallas import tpu as pltpu
 from jax.sharding import PartitionSpec as P
 
 
@@ -61,9 +65,224 @@
     return portion[None]
 
 
+MESH = pl.DeviceIdType.MESH
+LANES = 128
+CHUNKS = 4
+
+
+def fold_kernel(owners, gate_ref, up_ref, gain_ref, mix_ref, out_ref):
+    gain = gain_ref[...]
+    gate = (gate_ref[0].astype(jnp.float32) * gain).astype(jnp.bfloat16)
+    up = (up_ref[0].astype(jnp.float32) * gain).astype(jnp.bfloat16)
+    mix = mix_ref[...]
+    for u in range(gate.shape[1] // LANES):
+        both = jnp.concatenate(
+            (gate[:, u * LANES : (u + 1) * LANES], up[:, u * LANES : (u + 1) * LANES]), axis=1
+        )
+        out_ref[0, :, 2 * u * LANES : 2 * (u + 1) * LANES] = jnp.dot(
+            both, mix, preferred_element_type=jnp.float32
+        ).astype(jnp.bfloat16)
+
+
+def fold_slots(owners, gate, up, gain, slots):
+    _, rows, units = gate.shape
+    step = rows // 2
+    k = jnp.arange(2 * LANES)
+    mix = (k[None, :] == jnp.where(k < LANES, 2 * k, 2 * (k - LANES) + 1)[:, None]).astype(
+        jnp.bfloat16
+    )
+    spec = pl.BlockSpec((1, step, units), lambda s, i, owners: (owners[s], i, 0))
+    return pl.pallas_call(
+        fold_kernel,
+        out_shape=jax.ShapeDtypeStruct((slots, rows, 2 * units), jnp.bfloat16),
+        grid_spec=pltpu.PrefetchScalarGridSpec(
+            num_scalar_prefetch=1,
+            grid=(slots, rows // step),
+            in_specs=[
+                spec,
+                spec,
+                pl.BlockSpec((step, 1), lambda s, i, owners: (i, 0)),
+                pl.BlockSpec((2 * LANES, 2 * LANES), lambda s, i, owners: (0, 0)),
+            ],
+            out_specs=pl.BlockSpec((1, step, 2 * units), lambda s, i, owners: (s, i, 0)),
+        ),
+        compiler_params=pltpu.CompilerParams(vmem_limit_bytes=32 << 20),
+        name="fold",
+    )(owners, gate, up, gain[:, None], mix)
+
+
+def exchange_kernel(
+    n, chunks, mine, all_ref, s1s, s1r, ys, yr, c0s, c0r, c1s, c1r, own_sem
+):
+    f, r = lax.axis_index("fsdp"), lax.axis_index("rep")
+    r_core = r + 1 - 2 * (r % 2)
+    r_y = (r + 2) % 4
+    _, rows, width = mine.shape
+    size = rows // chunks
+
+    barrier = pltpu.get_barrier_semaphore()
+    for k in range(1, n):
+        pl.semaphore_signal(barrier, inc=1, device_id=((f + k) % n, r), device_id_type=MESH)
+    for other in (r_core, r_y):
+        pl.semaphore_signal(barrier, inc=1, device_id=(f, other), device_id_type=MESH)
+    pl.semaphore_wait(barrier, n + 1)
+
+    def row(ch):
+        return pl.ds(pl.multiple_of(ch * size, size), size)
+
+    def region(i, ch, q):
+        return all_ref.at[i, row(ch), pl.ds(pl.multiple_of(q * width, width), width)]
+
+    def send(src, dst, device, send_sem, recv_sem, at):
+        return pltpu.make_async_remote_copy(
+            src_ref=src,
+            dst_ref=dst,
+            send_sem=send_sem.at[at],
+            recv_sem=recv_sem.at[at],
+            device_id=device,
+            device_id_type=MESH,
+        )
+
+    def scatter(k, ch):
+        d = (f + k) % n
+        return send(mine.at[d, row(ch)], region(f, ch, r), (d, r), s1s, s1r, k * chunks + ch)
+
+    def over_y(src, k, ch):
+        return send(src, region((f + n - k) % n, ch, r), (f, r_y), ys, yr, k * chunks + ch)
+
+    def over_core(src, k, ch):
+        return send(src, region((f + n - k) % n, ch, r), (f, r_core), c0s, c0r, k * chunks + ch)
+
+    def y_to_core(k, ch):
+        part = region((f + n - k) % n, ch, r_y)
+        return send(part, part, (f, r_core), c1s, c1r, k * chunks + ch)
+
+    def held(k, ch):
+        return region((f + n - k) % n, ch, r)
+
+    def scatter_chunk(ch):
+        def body(k, _):
+            scatter(k, ch).start()
+            return 0
+
+        lax.fori_loop(1, n, body, 0)
+
+    own = pltpu.make_async_copy(
+        mine.at[f], all_ref.at[f, :, pl.ds(pl.multiple_of(r * width, width), width)], own_sem
+    )
+    scatter_chunk(0)
+
+    def own_out(ch, _):
+        over_y(mine.at[f, row(ch)], 0, ch).start()
+        over_core(mine.at[f, row(ch)], 0, ch).start()
+        return 0
+
+    lax.fori_loop(0, chunks, own_out, 0)
+
+    def later(ch, _):
+        scatter_chunk(ch)
+        return 0
+
+    lax.fori_loop(1, chunks, later, 0)
+    own.start()
+
+    def pass_on(k, ch):
+        over_y(held(k, ch), k, ch).wait_recv()
+        y_to_core(k, ch).start()
+
+    def step(t, _):
+        k, ch = 1 + t % (n - 1), t // (n - 1)
+        scatter(k, ch).wait_recv()
+        over_y(held(k, ch), k, ch).start()
+        over_core(held(k, ch), k, ch).start()
+
+        @pl.when(t < chunks)
+        def _():
+            pass_on(0, t)
+
+        @pl.when(t >= chunks)
+        def _():
+            u = t - chunks
+            pass_on(1 + u % (n - 1), u // (n - 1))
+
+        return 0
+
+    lax.fori_loop(0, (n - 1) * chunks, step, 0)
+
+    def last(t, _):
+        u = (n - 1) * chunks - chunks + t
+        pass_on(1 + u % (n - 1), u // (n - 1))
+        return 0
+
+    lax.fori_loop(0, chunks, last, 0)
+
+    def finish(t, _):
+        k, ch = t // chunks, t % chunks
+        over_core(held(k, ch), k, ch).wait_recv()
+        y_to_core(k, ch).wait_recv()
+        over_y(held(k, ch), k, ch).wait_send()
+        over_core(held(k, ch), k, ch).wait_send()
+        y_to_core(k, ch).wait_send()
+        return 0
+
+    lax.fori_loop(0, n * chunks, finish, 0)
+
+    def sent(t, _):
+        scatter(1 + t // chunks, t % chunks).wait_send()
+        return 0
+
+    lax.fori_loop(0, (n - 1) * chunks, sent, 0)
+    own.wait()
+
+
+def exchange(mine, n, reps):
+    _, rows, width = mine.shape
+    count = n * CHUNKS
+    return pl.pallas_call(
+        functools.partial(exchange_kernel, n, CHUNKS),
+        out_shape=jax.ShapeDtypeStruct((n, rows, reps * width), mine.dtype),
+        in_specs=[pl.BlockSpec(memory_space=pl.ANY)],
+        out_specs=pl.BlockSpec(memory_space=pl.ANY),
+        scratch_shapes=[pltpu.SemaphoreType.DMA((count,))] * 8 + [pltpu.SemaphoreType.DMA],
+        compiler_params=pltpu.CompilerParams(collective_id=0, has_side_effects=True),
+        name="exchange",
+    )(mine)
+
+
+def place_kernel(matching, in_ref, out_ref):
+    out_ref[...] = in_ref[0]
+
+
+def place(matching, blocks):
+    n, rows, width = blocks.shape
+    cut = 2
+    return pl.pallas_call(
+        place_kernel,
+        out_shape=jax.ShapeDtypeStruct((n * rows, width), blocks.dtype),
+        grid_spec=pltpu.PrefetchScalarGridSpec(
+            num_scalar_prefetch=1,
+            grid=(n, cut),
+            in_specs=[pl.BlockSpec((1, rows // cut, width), lambda i, j, matching: (i, j, 0))],
+            out_specs=pl.BlockSpec(
+                (rows // cut, width), lambda i, j, matching: (matching[i] * cut + j, 0)
+            ),
+        ),
+        compiler_params=pltpu.CompilerParams(vmem_limit_bytes=40 << 20),
+        name="place",
+    )(matching, blocks)
+
+
+def local_whole(gate_shards, up_shards, norm_gain, matching, replica_slots, replica_count):
+    n, reps = lax.axis_size("fsdp"), lax.axis_size("rep")
+    owners = slot_owner(replica_slots, replica_count, n)
+    mine = fold_slots(owners, gate_shards, up_shards, norm_gain, n)
+    return place(matching, exchange(mine, n, reps))[None]
+
+
 def solution(mesh):
+    whole_experts = mesh.shape["fsdp"] == 8 and mesh.shape["rep"] == 4
     return jax.shard_map(
-        local,
+        local_whole if whole_experts else local,
         mesh=mesh,
         in_specs=(P(None, "fsdp", "rep"), P(None, "fsdp", "rep"), P("fsdp"), P(), P(), P()),
         out_specs=P("fsdp", None, None),

time: 1940 us -> 467 us (0.24)
  blocking collectives: 1270 us -> 0 us
  Pallas kernels: 0 us -> 455 us
  local copies, waits for them, and re-layouts: 311 us -> 10.4 us
  waiting for transfers between devices: 158 us -> 0 us
  other arithmetic: 158 us -> 1.6 us
    all_gather x1 -> x0, blocking collectives: 1270 us -> none  [local(): gain_all = lax.all_gather(norm_gain, 'fsdp', axis=0, tiled=True)]
    pallas_call x0 -> x3, Pallas kernels: none -> 455 us  [the longest x1 405 us: exchange(): pl.pallas_call(functools.partial(exchange_kernel, n, CHUNKS), out_shape=j...]
    all_gather x2 -> x0, waiting for transfers between devices: 157 us -> none  [the longest x1 94.4 us: local(): lax.all_gather(gate_shards, 'rep', axis=2, tiled=True)]
    gather x13 -> x0, local copies, waits for them, and re-layouts: 156 us -> none  [the longest x5 90.8 us: local(): portion = received[inverse].reshape(devices * rows, received.shape[2])]
    another operation x1 -> x0, local copies, waits for them, and re-layouts: 80.1 us -> none  [alternate(): jnp.stack((gate_part, up_part), axis=-1)]
    another operation x2 -> x0, other arithmetic: 77.8 us -> none  [alternate(): jnp.stack((gate_part, up_part), axis=-1)]
    reshape x1 -> x0, local copies, waits for them, and re-layouts: 74.2 us -> none  [alternate(): jnp.stack((gate_part, up_part), axis=-1)]
    convert_element_type x1, other arithmetic: 39.3 us -> 0.1 us  [fold_slots(): (k[None, :] == jnp.where(k < LANES, 2 * k, 2 * (k - LANES) + 1)[:, None])...]
  transfers between devices with their start and end apart: 3 -> 0, of which waited for: 2 -> 0; matrix products, arithmetic and copies ran while one was open for 2% -> 0% of each run, Pallas kernels for 0% -> 0%
where the time goes in v1:
time: 467 us
  Pallas kernels  455 us (97%)
  local copies, waits for them, and re-layouts  10.4 us (2%)
    pallas_call x1, Pallas kernels, exchange(): pl.pallas_call(functools.partial(exchange_kernel, n, CHUNKS), out_shape=j...  405 us
    pallas_call x1, Pallas kernels, place(): pl.pallas_call(place_kernel, out_shape=jax.ShapeDtypeStruct((n * rows, wi...  41.5 us
    unnamed x8, local copies, waits for them, and re-layouts  9.54 us

profile of v1, /device:TPU:9, one launch (start us, length us, event | category | flops | bytes accessed | tf_op | source)
XLA Modules:
  0.0 466.9 jit_solution(159448207804395453)
XLA Ops:
  0.0 0.7 iota_compare_fusion.3
  0.7 0.8 select_reduce_fusion.owners
  1.5 0.1 fusion.mix_ref
  1.6 0.9 broadcast_in_dim.6.gain_ref
  2.5 0.0 copy-start.1
  2.5 2.0 copy-done.1
  4.5 0.0 copy-start.2
  4.5 2.0 copy-done.2
  6.6 7.9 %fold.1.mine = bf16[8,896,1024]{2,1,0:T(8,128)(2,1)S(1)} custom-call(s32[8]{0:T(128)S(1)} %select_reduce_fusion.owners, bf16[4,896,512]{2,1,0:T(8,128)(2,1)S(1)} %copy-done.1, bf16[4,896,512]{2,1,0:T(8,128)(2,1)S(1)} %copy-done.2, f32[896,1]{1,0:T(8,128)S(1)} %broadcast_in_dim.6.gain_ref, bf16[256,256]{1,0:T(8,128)(2,1)S(1)} %fusion.mix_ref), custom_call_target="tpu_custom_call" | custom-call | tf_op jit(solution)/shard_map/fold/pallas_call | solution.py:95
  14.5 0.0 copy-start
  14.5 5.5 %copy-done = bf16[8,896,1024]{2,1,0:T(8,128)(2,1)} copy-done((bf16[8,896,1024]{2,1,0:T(8,128)(2,1)}, bf16[8,896,1024]{2,1,0:T(8,128)(2,1)S(1)}, u32[]{:S(2)}) %copy-start) | copy-done | bytes 14680088
  20.0 0.0 copy-start.3
  20.0 405.4 %exchange.1.in_ref = bf16[8,896,4096]{2,1,0:T(8,128)(2,1)} custom-call(bf16[8,896,1024]{2,1,0:T(8,128)(2,1)} %copy-done), custom_call_target="tpu_custom_call" | custom-call | tf_op jit(solution)/shard_map/exchange/pallas_call | solution.py:241
  425.4 0.0 copy-done.3
  425.4 41.5 %place.1 = bf16[7168,4096]{1,0:T(8,128)(2,1)} custom-call(s32[8]{0:T(128)S(1)} %copy-done.3, bf16[8,896,4096]{2,1,0:T(8,128)(2,1)} %exchange.1.in_ref), custom_call_target="tpu_custom_call" | custom-call | tf_op jit(solution)/shard_map/place/pallas_call | solution.py:259
  (1 shorter events, 0.0 us)
Async XLA Ops:
  2.5 2.0 copy-start.1
  4.5 2.0 copy-start.2
  14.5 5.5 %copy-start = (bf16[8,896,1024]{2,1,0:T(8,128)(2,1)}, bf16[8,896,1024]{2,1,0:T(8,128)(2,1)S(1)}, u32[]{:S(2)}) copy-start(bf16[8,896,1024]{2,1,0:T(8,128)(2,1)S(1)} %fold.1.mine) | copy-start | bytes 44040196
  20.0 405.4 %copy-start.3 = (s32[8]{0:T(128)S(1)}, s32[8]{0:T(128)}, u32[]{:S(2)}) copy-start(s32[8]{0:T(128)} %matching.1) | copy-start | bytes 100

commit v2 on v1

--- a/solution.py
+++ b/solution.py
@@ -67,7 +67,8 @@
 
 MESH = pl.DeviceIdType.MESH
 LANES = 128
-CHUNKS = 4
+CHUNKS = 8
+ROUNDS = 2
 
 
 def fold_kernel(owners, gate_ref, up_ref, gain_ref, mix_ref, out_ref):
@@ -106,7 +107,7 @@
             ],
             out_specs=pl.BlockSpec((1, step, 2 * units), lambda s, i, owners: (s, i, 0)),
         ),
-        compiler_params=pltpu.CompilerParams(vmem_limit_bytes=32 << 20),
+        compiler_params=pltpu.CompilerParams(vmem_limit_bytes=56 << 20),
         name="fold",
     )(owners, gate, up, gain[:, None], mix)
 
@@ -160,17 +161,19 @@
     def held(k, ch):
         return region((f + n - k) % n, ch, r)
 
-    def scatter_chunk(ch):
-        def body(k, _):
-            scatter(k, ch).start()
-            return 0
-
-        lax.fori_loop(1, n, body, 0)
+    window = ROUNDS * (n - 1)
+
+    def scatter_at(t):
+        return scatter(1 + t % (n - 1), t // (n - 1))
+
+    def begin(t, _):
+        scatter_at(t).start()
+        return 0
 
     own = pltpu.make_async_copy(
         mine.at[f], all_ref.at[f, :, pl.ds(pl.multiple_of(r * width, width), width)], own_sem
     )
-    scatter_chunk(0)
+    lax.fori_loop(0, n - 1, begin, 0)
 
     def own_out(ch, _):
         over_y(mine.at[f, row(ch)], 0, ch).start()
@@ -179,11 +182,7 @@
 
     lax.fori_loop(0, chunks, own_out, 0)
 
-    def later(ch, _):
-        scatter_chunk(ch)
-        return 0
-
-    lax.fori_loop(1, chunks, later, 0)
+    lax.fori_loop(n - 1, window, begin, 0)
     own.start()
 
     def pass_on(k, ch):
@@ -195,6 +194,11 @@
         scatter(k, ch).wait_recv()
         over_y(held(k, ch), k, ch).start()
         over_core(held(k, ch), k, ch).start()
+        scatter(k, ch).wait_send()
+
+        @pl.when(t < (n - 1) * chunks - window)
+        def _():
+            scatter_at(t + window).start()
 
         @pl.when(t < chunks)
         def _():
@@ -227,11 +231,6 @@
 
     lax.fori_loop(0, n * chunks, finish, 0)
 
-    def sent(t, _):
-        scatter(1 + t // chunks, t % chunks).wait_send()
-        return 0
-
-    lax.fori_loop(0, (n - 1) * chunks, sent, 0)
     own.wait()
 
 
@@ -249,25 +248,37 @@
     )(mine)
 
 
-def place_kernel(matching, in_ref, out_ref):
-    out_ref[...] = in_ref[0]
+def place_kernel(cut, matching, in_ref, out_ref, sems):
+    n, rows, _ = in_ref.shape
+    size = rows // cut
+
+    def piece(i, j):
+        return pltpu.make_async_copy(
+            in_ref.at[i, pl.ds(j * size, size)],
+            out_ref.at[pl.ds(pl.multiple_of(matching[i] * rows + j * size, size), size)],
+            sems.at[i, j],
+        )
+
+    for i in range(n):
+        for j in range(cut):
+            piece(i, j).start()
+    for i in range(n):
+        for j in range(cut):
+            piece(i, j).wait()
 
 
 def place(matching, blocks):
     n, rows, width = blocks.shape
-    cut = 2
+    cut = 4
     return pl.pallas_call(
-        place_kernel,
+        functools.partial(place_kernel, cut),
         out_shape=jax.ShapeDtypeStruct((n * rows, width), blocks.dtype),
-        grid_spec=pltpu.PrefetchScalarGridSpec(
-            num_scalar_prefetch=1,
-            grid=(n, cut),
-            in_specs=[pl.BlockSpec((1, rows // cut, width), lambda i, j, matching: (i, j, 0))],
-            out_specs=pl.BlockSpec(
-                (rows // cut, width), lambda i, j, matching: (matching[i] * cut + j, 0)
-            ),
-        ),
-        compiler_params=pltpu.CompilerParams(vmem_limit_bytes=40 << 20),
+        in_specs=[
+            pl.BlockSpec(memory_space=pltpu.SMEM),
+            pl.BlockSpec(memory_space=pl.ANY),
+        ],
+        out_specs=pl.BlockSpec(memory_space=pl.ANY),
+        scratch_shapes=[pltpu.SemaphoreType.DMA((n, cut))],
         name="place",
     )(matching, blocks)
 

time: 467 us -> 2170 us (4.65)
  Pallas kernels: 455 us -> 2170 us
    pallas_call x1, Pallas kernels: 41.5 us -> 1780 us  [place(): pl.pallas_call(functools.partial(place_kernel, cut), out_shape=jax.ShapeD...]
    pallas_call x1, Pallas kernels: 405 us -> 367 us  [exchange(): pl.pallas_call(functools.partial(exchange_kernel, n, CHUNKS), out_shape=j...]
where the time goes in v2:
time: 2170 us
  Pallas kernels  2170 us (100%)
    pallas_call x1, Pallas kernels, place(): pl.pallas_call(functools.partial(place_kernel, cut), out_shape=jax.ShapeD...  1780 us
    pallas_call x1, Pallas kernels, exchange(): pl.pallas_call(functools.partial(exchange_kernel, n, CHUNKS), out_shape=j...  367 us

profile of v2, /device:TPU:9, one launch (start us, length us, event | category | flops | bytes accessed | tf_op | source)
XLA Modules:
  0.0 2172.8 jit_solution(3749125037734953650)
XLA Ops:
  0.0 0.7 iota_compare_fusion.3
  0.7 1.3 select_reduce_fusion.owners
  2.0 0.8 fusion.mix_ref
  2.8 1.6 broadcast_in_dim.6.gain_ref
  4.4 20.4 fold.1.mine
  24.8 367.1 %exchange.1.in_ref = bf16[8,896,4096]{2,1,0:T(8,128)(2,1)} custom-call(bf16[8,896,1024]{2,1,0:T(8,128)(2,1)} %fold.1.mine), custom_call_target="tpu_custom_call" | custom-call | tf_op jit(solution)/shard_map/exchange/pallas_call | solution.py:240
  391.9 1780.9 %place.1 = bf16[7168,4096]{1,0:T(8,128)(2,1)} custom-call(s32[8]{0:T(128)} %matching.1, bf16[8,896,4096]{2,1,0:T(8,128)(2,1)} %exchange.1.in_ref), custom_call_target="tpu_custom_call" | custom-call | tf_op jit(solution)/shard_map/place/pallas_call | solution.py:273
  (1 shorter events, 0.0 us)

commit v3 on v2

v3 whole, which is shorter than its diff:
```python
import functools

import jax
import jax.numpy as jnp
from jax import lax
from jax.experimental import pallas as pl
from jax.experimental.pallas import tpu as pltpu
from jax.sharding import PartitionSpec as P


def slot_owner(replica_slots, replica_count, slots):
    live = jnp.arange(replica_slots.shape[1])[None, :] < replica_count[:, None]
    hits = live[:, :, None] & (replica_slots[:, :, None] == jnp.arange(slots)[None, None, :])
    owners = jnp.arange(replica_slots.shape[0], dtype=jnp.int32)[:, None, None] * hits.astype(
        jnp.int32
    )
    return jnp.sum(owners, axis=(0, 1))


def inverse_order(matching):
    count = matching.shape[0]
    match_grid = matching[None, :] == jnp.arange(count, dtype=jnp.int32)[:, None]
    ranks = jnp.where(match_grid, jnp.arange(count, dtype=jnp.int32)[None, :], 0)
    return jnp.sum(ranks, axis=1)


def fold_rows(weights, gain_rows):
    return (weights.astype(jnp.float32) * gain_rows[:, None]).astype(jnp.bfloat16)


def pick_units(weights, expert_pick, block_pick, block_count):
    experts, rows, units = weights.shape
    return weights.reshape(experts, rows, units // block_count, block_count)[
        expert_pick, :, :, block_pick
    ]


def alternate(gate_part, up_part):
    shape = gate_part.shape
    return jnp.stack((gate_part, up_part), axis=-1).reshape(shape[:-1] + (2 * shape[-1],))


def local(gate_shards, up_shards, norm_gain, matching, replica_slots, replica_count):
    devices = lax.axis_size("fsdp")
    block_count = min(8, devices // 8)
    rows = gate_shards.shape[1]
    owners = slot_owner(replica_slots, replica_count, devices // block_count)
    targets = jnp.arange(devices, dtype=jnp.int32)
    expert_pick = owners[targets // block_count]
    block_pick = targets % block_count
    inverse = inverse_order(matching)
    gate_all, up_all = (
        lax.all_gather(gate_shards, "rep", axis=2, tiled=True),
        lax.all_gather(up_shards, "rep", axis=2, tiled=True),
    )
    outgoing = alternate(
        pick_units(gate_all, expert_pick, block_pick, block_count),
        pick_units(up_all, expert_pick, block_pick, block_count),
    )
    received = lax.all_to_all(outgoing, "fsdp", split_axis=0, concat_axis=0, tiled=True)
    portion = received[inverse].reshape(devices * rows, received.shape[2])
    gain_all = lax.all_gather(norm_gain, "fsdp", axis=0, tiled=True)
    gain_model = gain_all.reshape(devices, rows)[inverse].reshape(devices * rows)
    portion = fold_rows(portion, gain_model)
    return portion[None]


MESH = pl.DeviceIdType.MESH
LANES = 128
CHUNKS = 8
ROUNDS = 2


def exchange_kernel(
    n,
    chunks,
    owners,
    gain_ref,
    gate_hbm,
    up_hbm,
    all_ref,
    gate,
    up,
    mix,
    mine,
    s1s,
    s1r,
    ys,
    yr,
    c0s,
    c0r,
    c1s,
    c1r,
    gate_sem,
    up_sem,
    own_sem,
):
    f, r = lax.axis_index("fsdp"), lax.axis_index("rep")
    r_core = r + 1 - 2 * (r % 2)
    r_y = (r + 2) % 4
    _, rows, width = mine.shape
    size = rows // chunks

    def row(ch):
        return pl.ds(pl.multiple_of(ch * size, size), size)

    def load(ch):
        return (
            pltpu.make_async_copy(gate_hbm.at[:, row(ch)], gate.at[:, row(ch)], gate_sem.at[ch]),
            pltpu.make_async_copy(up_hbm.at[:, row(ch)], up.at[:, row(ch)], up_sem.at[ch]),
        )

    def begin_load(ch, _):
        for copy in load(ch):
            copy.start()
        return 0

    lax.fori_loop(0, chunks, begin_load, 0)

    def mate(k):
        total, bit = 0, 1
        while bit < n:
            total = total + (f // bit + k // bit) % 2 * bit
            bit *= 2
        return total

    barrier = pltpu.get_barrier_semaphore()
    for k in range(1, n):
        pl.semaphore_signal(barrier, inc=1, device_id=(mate(k), r), device_id_type=MESH)
    for other in (r_core, r_y):
        pl.semaphore_signal(barrier, inc=1, device_id=(f, other), device_id_type=MESH)

    source = lax.broadcasted_iota(jnp.int32, mix.shape, 0)
    target = lax.broadcasted_iota(jnp.int32, mix.shape, 1)
    place_of = jnp.where(source < LANES, 2 * source, 2 * source - (2 * LANES - 1))
    mix[...] = jnp.where(place_of == target, 1.0, 0.0).astype(jnp.bfloat16)

    def fold(d, ch):
        e = owners[d]
        gain = gain_ref[row(ch), :]
        g = (gate[e, row(ch), :].astype(jnp.float32) * gain).astype(jnp.bfloat16)
        u = (up[e, row(ch), :].astype(jnp.float32) * gain).astype(jnp.bfloat16)
        for c in range(0, g.shape[1], LANES):
            both = jnp.concatenate((g[:, c : c + LANES], u[:, c : c + LANES]), axis=1)
            mine[d, row(ch), 2 * c : 2 * (c + LANES)] = jnp.dot(
                both, mix[...], preferred_element_type=jnp.float32
            ).astype(jnp.bfloat16)

    def region(i, ch, q):
        return all_ref.at[i, row(ch), pl.ds(pl.multiple_of(q * width, width), width)]

    def send(src, dst, device, send_sem, recv_sem, at):
        return pltpu.make_async_remote_copy(
            src_ref=src,
            dst_ref=dst,
            send_sem=send_sem.at[at],
            recv_sem=recv_sem.at[at],
            device_id=device,
            device_id_type=MESH,
        )

    def scatter(k, ch):
        d = mate(k)
        return send(mine.at[d, row(ch)], region(f, ch, r), (d, r), s1s, s1r, k * chunks + ch)

    def over_y(src, k, ch):
        return send(src, region(mate(k), ch, r), (f, r_y), ys, yr, k * chunks + ch)

    def over_core(src, k, ch):
        return send(src, region(mate(k), ch, r), (f, r_core), c0s, c0r, k * chunks + ch)

    def y_to_core(k, ch):
        part = region(mate(k), ch, r_y)
        return send(part, part, (f, r_core), c1s, c1r, k * chunks + ch)

    def held(k, ch):
        return region(mate(k), ch, r)

    window = ROUNDS * (n - 1)

    def at(t):
        p = t % (n - 1)
        return (p + 1) // 2 + (p + 1) % 2 * (n // 2), t // (n - 1)

    def begin(t, _):
        k, ch = at(t)
        fold(mate(k), ch)
        scatter(k, ch).start()
        return 0

    def loaded(ch, _):
        for copy in load(ch):
            copy.wait()
        return 0

    lax.fori_loop(0, chunks, loaded, 0)
    pl.semaphore_wait(barrier, n + 1)
    lax.fori_loop(0, n - 1, begin, 0)

    def own_out(ch, _):
        fold(f, ch)
        over_y(mine.at[f, row(ch)], 0, ch).start()
        over_core(mine.at[f, row(ch)], 0, ch).start()
        return 0

    lax.fori_loop(0, chunks, own_out, 0)
    lax.fori_loop(n - 1, window, begin, 0)
    own = pltpu.make_async_copy(
        mine.at[f], all_ref.at[f, :, pl.ds(pl.multiple_of(r * width, width), width)], own_sem
    )
    own.start()

    def pass_on(k, ch):
        over_y(held(k, ch), k, ch).wait_recv()
        y_to_core(k, ch).start()

    def step(t, _):
        k, ch = at(t)
        scatter(k, ch).wait_recv()
        over_y(held(k, ch), k, ch).start()
        over_core(held(k, ch), k, ch).start()
        scatter(k, ch).wait_send()

        @pl.when(t < (n - 1) * chunks - window)
        def _():
            begin(t + window, 0)

        @pl.when(t < chunks)
        def _():
            pass_on(0, t)

        @pl.when(t >= chunks)
        def _():
            pass_on(*at(t - chunks))

        return 0

    lax.fori_loop(0, (n - 1) * chunks, step, 0)

    def last(t, _):
        pass_on(*at(t))
        return 0

    lax.fori_loop((n - 2) * chunks, (n - 1) * chunks, last, 0)

    def finish(t, _):
        k, ch = t // chunks, t % chunks
        over_core(held(k, ch), k, ch).wait_recv()
        y_to_core(k, ch).wait_recv()
        over_y(held(k, ch), k, ch).wait_send()
        over_core(held(k, ch), k, ch).wait_send()
        y_to_core(k, ch).wait_send()
        return 0

    lax.fori_loop(0, n * chunks, finish, 0)
    own.wait()


def exchange(owners, gate, up, gain, n, reps):
    _, rows, units = gate.shape
    count = n * CHUNKS
    return pl.pallas_call(
        functools.partial(exchange_kernel, n, CHUNKS),
        out_shape=jax.ShapeDtypeStruct((n, rows, reps * 2 * units), gate.dtype),
        in_specs=[
            pl.BlockSpec(memory_space=pltpu.SMEM),
            pl.BlockSpec(memory_space=pltpu.VMEM),
            pl.BlockSpec(memory_space=pl.ANY),
            pl.BlockSpec(memory_space=pl.ANY),
        ],
        out_specs=pl.BlockSpec(memory_space=pl.ANY),
        scratch_shapes=[
            pltpu.VMEM(gate.shape, gate.dtype),
            pltpu.VMEM(up.shape, up.dtype),
            pltpu.VMEM((2 * LANES, 2 * LANES), gate.dtype),
            pltpu.VMEM((n, rows, 2 * units), gate.dtype),
        ]
        + [pltpu.SemaphoreType.DMA((count,))] * 8
        + [pltpu.SemaphoreType.DMA((CHUNKS,))] * 2
        + [pltpu.SemaphoreType.DMA],
        compiler_params=pltpu.CompilerParams(
            collective_id=0, has_side_effects=True, vmem_limit_bytes=56 << 20
        ),
        name="exchange",
    )(owners, gain[:, None], gate, up)


def place_kernel(cut, slots, matching, in_ref, out_ref, ring, in_sems, out_sems):
    n, rows, _ = in_ref.shape
    size = rows // cut
    pieces = n * cut

    def bring(p):
        return pltpu.make_async_copy(
            in_ref.at[p // cut, pl.ds(p % cut * size, size)],
            ring.at[p % slots],
            in_sems.at[p % slots],
        )

    def put(p):
        start = pl.multiple_of(matching[p // cut] * rows + p % cut * size, size)
        return pltpu.make_async_copy(
            ring.at[p % slots], out_ref.at[pl.ds(start, size)], out_sems.at[p % slots]
        )

    for p in range(slots):
        bring(p).start()
    for p in range(pieces):
        bring(p).wait()
        put(p).start()
        done = p - slots // 2
        if done >= 0 and done + slots < pieces:
            put(done).wait()
            bring(done + slots).start()
    for p in range(pieces - slots, pieces):
        put(p).wait()


def place(matching, blocks):
    n, rows, width = blocks.shape
    cut, slots = 4, 16
    return pl.pallas_call(
        functools.partial(place_kernel, cut, slots),
        out_shape=jax.ShapeDtypeStruct((n * rows, width), blocks.dtype),
        in_specs=[
            pl.BlockSpec(memory_space=pltpu.SMEM),
            pl.BlockSpec(memory_space=pl.ANY),
        ],
        out_specs=pl.BlockSpec(memory_space=pl.ANY),
        scratch_shapes=[
            pltpu.VMEM((slots, rows // cut, width), blocks.dtype),
            pltpu.SemaphoreType.DMA((slots,)),
            pltpu.SemaphoreType.DMA((slots,)),
        ],
        compiler_params=pltpu.CompilerParams(vmem_limit_bytes=40 << 20),
        name="place",
    )(matching, blocks)


def local_whole(gate_shards, up_shards, norm_gain, matching, replica_slots, replica_count):
    n, reps = lax.axis_size("fsdp"), lax.axis_size("rep")
    owners = slot_owner(replica_slots, replica_count, n)
    blocks = exchange(owners, gate_shards, up_shards, norm_gain, n, reps)
    return place(matching, blocks)[None]


def solution(mesh):
    whole_experts = mesh.shape["fsdp"] == 8 and mesh.shape["rep"] == 4
    return jax.shard_map(
        local_whole if whole_experts else local,
        mesh=mesh,
        in_specs=(P(None, "fsdp", "rep"), P(None, "fsdp", "rep"), P("fsdp"), P(), P(), P()),
        out_specs=P("fsdp", None, None),
        check_vma=False,
    )
```

time: 2170 us -> 414 us (0.19)
  Pallas kernels: 2170 us -> 409 us
    pallas_call x2 -> x1, Pallas kernels: 1800 us -> 39.5 us  [place(): pl.pallas_call(functools.partial(place_kernel, cut, slots), out_shape=jax...]
where the time goes in v3:
time: 414 us; the launch traced here: 413 us
  Pallas kernels  409 us (99%)
    pallas_call x1, Pallas kernels, exchange(): pl.pallas_call(functools.partial(exchange_kernel, n, CHUNKS), out_shape=j...  370 us
    pallas_call x1, Pallas kernels, place(): pl.pallas_call(functools.partial(place_kernel, cut, slots), out_shape=jax...  39.5 us

profile of v3, /device:TPU:9, one launch (start us, length us, event | category | flops | bytes accessed | tf_op | source)
XLA Modules:
  0.0 412.9 jit_solution(10074105231946442136)
XLA Ops:
  0.0 0.0 copy-start
  0.0 0.7 iota_compare_fusion.1
  0.7 1.3 select_reduce_fusion.owners
  2.1 1.6 broadcast_in_dim.6.gain_ref
  3.7 369.7 %exchange.1.in_ref = bf16[8,896,4096]{2,1,0:T(8,128)(2,1)} custom-call(s32[8]{0:T(128)} %select_reduce_fusion.owners, f32[896,1]{1,0:T(8,128)} %broadcast_in_dim.6.gain_ref, bf16[4,896,512]{2,1,0:T(8,128)(2,1)} %gate_hbm.1, bf16[4,896,512]{2,1,0:T(8,128)(2,1)} %up_hbm.1), custom_call_target="tpu_custom_call" | custom-call | tf_op jit(solution)/shard_map/exchange/pallas_call | solution.py:262
  373.4 0.0 copy-done
  373.4 39.5 %place.1 = bf16[7168,4096]{1,0:T(8,128)(2,1)} custom-call(s32[8]{0:T(128)S(1)} %copy-done, bf16[8,896,4096]{2,1,0:T(8,128)(2,1)} %exchange.1.in_ref), custom_call_target="tpu_custom_call" | custom-call | tf_op jit(solution)/shard_map/place/pallas_call | solution.py:322
Async XLA Ops:
  0.0 373.4 %copy-start = (s32[8]{0:T(128)S(1)}, s32[8]{0:T(128)}, u32[]{:S(2)}) copy-start(s32[8]{0:T(128)} %matching.1) | copy-start | bytes 100

commit v4 on v3

--- a/solution.py
+++ b/solution.py
@@ -79,6 +79,7 @@
     gate_hbm,
     up_hbm,
     all_ref,
+    near_ref,
     gate,
     up,
     mix,
@@ -146,8 +147,8 @@
                 both, mix[...], preferred_element_type=jnp.float32
             ).astype(jnp.bfloat16)
 
-    def region(i, ch, q):
-        return all_ref.at[i, row(ch), pl.ds(pl.multiple_of(q * width, width), width)]
+    def region(i, ch, half):
+        return all_ref.at[i, row(ch), pl.ds(half * width, width)]
 
     def send(src, dst, device, send_sem, recv_sem, at):
         return pltpu.make_async_remote_copy(
@@ -161,20 +162,21 @@
 
     def scatter(k, ch):
         d = mate(k)
-        return send(mine.at[d, row(ch)], region(f, ch, r), (d, r), s1s, s1r, k * chunks + ch)
+        return send(mine.at[d, row(ch)], region(f, ch, 0), (d, r), s1s, s1r, k * chunks + ch)
 
     def over_y(src, k, ch):
-        return send(src, region(mate(k), ch, r), (f, r_y), ys, yr, k * chunks + ch)
+        return send(src, region(mate(k), ch, 1), (f, r_y), ys, yr, k * chunks + ch)
 
     def over_core(src, k, ch):
-        return send(src, region(mate(k), ch, r), (f, r_core), c0s, c0r, k * chunks + ch)
+        part = near_ref.at[0, mate(k), row(ch)]
+        return send(src, part, (f, r_core), c0s, c0r, k * chunks + ch)
 
     def y_to_core(k, ch):
-        part = region(mate(k), ch, r_y)
-        return send(part, part, (f, r_core), c1s, c1r, k * chunks + ch)
+        part = near_ref.at[1, mate(k), row(ch)]
+        return send(region(mate(k), ch, 1), part, (f, r_core), c1s, c1r, k * chunks + ch)
 
     def held(k, ch):
-        return region(mate(k), ch, r)
+        return region(mate(k), ch, 0)
 
     window = ROUNDS * (n - 1)
 
@@ -205,9 +207,7 @@
 
     lax.fori_loop(0, chunks, own_out, 0)
     lax.fori_loop(n - 1, window, begin, 0)
-    own = pltpu.make_async_copy(
-        mine.at[f], all_ref.at[f, :, pl.ds(pl.multiple_of(r * width, width), width)], own_sem
-    )
+    own = pltpu.make_async_copy(mine.at[f], all_ref.at[f, :, pl.ds(0, width)], own_sem)
     own.start()
 
     def pass_on(k, ch):
@@ -225,13 +225,13 @@
         def _():
             begin(t + window, 0)
 
-        @pl.when(t < chunks)
+        @pl.when((t >= chunks) & (t < 2 * chunks))
         def _():
-            pass_on(0, t)
-
-        @pl.when(t >= chunks)
+            pass_on(0, t - chunks)
+
+        @pl.when(t >= 2 * chunks)
         def _():
-            pass_on(*at(t - chunks))
+            pass_on(*at(t - 2 * chunks))
 
         return 0
 
@@ -241,7 +241,7 @@
         pass_on(*at(t))
         return 0
 
-    lax.fori_loop((n - 2) * chunks, (n - 1) * chunks, last, 0)
+    lax.fori_loop((n - 3) * chunks, (n - 1) * chunks, last, 0)
 
     def finish(t, _):
         k, ch = t // chunks, t % chunks
@@ -261,14 +261,20 @@
     count = n * CHUNKS
     return pl.pallas_call(
         functools.partial(exchange_kernel, n, CHUNKS),
-        out_shape=jax.ShapeDtypeStruct((n, rows, reps * 2 * units), gate.dtype),
+        out_shape=(
+            pltpu.HBM((n, rows, reps * units), gate.dtype),
+            pltpu.VMEM((2, n, rows, 2 * units), gate.dtype),
+        ),
         in_specs=[
             pl.BlockSpec(memory_space=pltpu.SMEM),
             pl.BlockSpec(memory_space=pltpu.VMEM),
             pl.BlockSpec(memory_space=pl.ANY),
             pl.BlockSpec(memory_space=pl.ANY),
         ],
-        out_specs=pl.BlockSpec(memory_space=pl.ANY),
+        out_specs=(
+            pl.BlockSpec(memory_space=pl.ANY),
+            pl.BlockSpec(memory_space=pltpu.VMEM),
+        ),
         scratch_shapes=[
             pltpu.VMEM(gate.shape, gate.dtype),
             pltpu.VMEM(up.shape, up.dtype),
@@ -279,33 +285,57 @@
         + [pltpu.SemaphoreType.DMA((CHUNKS,))] * 2
         + [pltpu.SemaphoreType.DMA],
         compiler_params=pltpu.CompilerParams(
-            collective_id=0, has_side_effects=True, vmem_limit_bytes=56 << 20
+            collective_id=0, has_side_effects=True, vmem_limit_bytes=26 << 20
         ),
         name="exchange",
     )(owners, gain[:, None], gate, up)
 
 
-def place_kernel(cut, slots, matching, in_ref, out_ref, ring, in_sems, out_sems):
-    n, rows, _ = in_ref.shape
+def place_kernel(
+    cut, slots, matching, in_ref, near_ref, out_ref, ring, in_sems, out_sems, sems
+):
+    r = lax.axis_index("rep")
+    r_core = r + 1 - 2 * (r % 2)
+    _, n, rows, width = near_ref.shape
     size = rows // cut
-    pieces = n * cut
+    pieces = 2 * n * cut
+
+    def target(i, start, count, q):
+        first = pl.multiple_of(matching[i] * rows + start, count)
+        return out_ref.at[
+            pl.ds(first, count), pl.ds(pl.multiple_of(q * width, width), width)
+        ]
+
+    def split(p):
+        return p // (2 * cut), p // 2 % cut * size, p % 2
 
     def bring(p):
+        i, start, half = split(p)
         return pltpu.make_async_copy(
-            in_ref.at[p // cut, pl.ds(p % cut * size, size)],
+            in_ref.at[i, pl.ds(start, size), pl.ds(half * width, width)],
             ring.at[p % slots],
             in_sems.at[p % slots],
         )
 
     def put(p):
-        start = pl.multiple_of(matching[p // cut] * rows + p % cut * size, size)
+        i, start, half = split(p)
         return pltpu.make_async_copy(
-            ring.at[p % slots], out_ref.at[pl.ds(start, size)], out_sems.at[p % slots]
+            ring.at[p % slots],
+            target(i, start, size, (r + 2 * half) % 4),
+            out_sems.at[p % slots],
+        )
+
+    def whole(i, far):
+        return pltpu.make_async_copy(
+            near_ref.at[far, i], target(i, 0, rows, (r_core + 2 * far) % 4), sems.at[i, far]
         )
 
     for p in range(slots):
         bring(p).start()
     for p in range(pieces):
+        if p % (2 * cut) == 0:
+            for far in range(2):
+                whole(p // (2 * cut), far).start()
         bring(p).wait()
         put(p).start()
         done = p - slots // 2
@@ -314,16 +344,20 @@
             bring(done + slots).start()
     for p in range(pieces - slots, pieces):
         put(p).wait()
-
-
-def place(matching, blocks):
-    n, rows, width = blocks.shape
-    cut, slots = 4, 16
+    for i in range(n):
+        for far in range(2):
+            whole(i, far).wait()
+
+
+def place(matching, blocks, near_blocks, reps):
+    _, n, rows, width = near_blocks.shape
+    cut, slots = 2, 16
     return pl.pallas_call(
         functools.partial(place_kernel, cut, slots),
-        out_shape=jax.ShapeDtypeStruct((n * rows, width), blocks.dtype),
+        out_shape=jax.ShapeDtypeStruct((n * rows, reps * width), blocks.dtype),
         in_specs=[
             pl.BlockSpec(memory_space=pltpu.SMEM),
+            pl.BlockSpec(memory_space=pltpu.HBM),
             pl.BlockSpec(memory_space=pl.ANY),
         ],
         out_specs=pl.BlockSpec(memory_space=pl.ANY),
@@ -331,17 +365,19 @@
             pltpu.VMEM((slots, rows // cut, width), blocks.dtype),
             pltpu.SemaphoreType.DMA((slots,)),
             pltpu.SemaphoreType.DMA((slots,)),
+            pltpu.SemaphoreType.DMA((n, 2)),
         ],
-        compiler_params=pltpu.CompilerParams(vmem_limit_bytes=40 << 20),
+        compiler_params=pltpu.CompilerParams(vmem_limit_bytes=32 << 20),
         name="place",
-    )(matching, blocks)
+    )(matching, blocks, near_blocks)
 
 
 def local_whole(gate_shards, up_shards, norm_gain, matching, replica_slots, replica_count):
     n, reps = lax.axis_size("fsdp"), lax.axis_size("rep")
     owners = slot_owner(replica_slots, replica_count, n)
-    blocks = exchange(owners, gate_shards, up_shards, norm_gain, n, reps)
-    return place(matching, blocks)[None]
+    parts = exchange(owners, gate_shards, up_shards, norm_gain, n, reps)
+    near = pltpu.with_memory_space_constraint(parts[1], pltpu.VMEM)
+    return place(matching, parts[0], near, reps)[None]
 
 
 def solution(mesh):

time: 414 us -> 405 us (0.978)
  Pallas kernels: 409 us -> 400 us
    pallas_call x1, Pallas kernels: 39.5 us -> 29.9 us  [place(): pl.pallas_call(functools.partial(place_kernel, cut, slots), out_shape=jax...]
where the time goes in v4:
time: 405 us; the launch traced here: 403 us
  Pallas kernels  400 us (99%)
    pallas_call x1, Pallas kernels, exchange(): pl.pallas_call(functools.partial(exchange_kernel, n, CHUNKS), out_shape=(...  370 us
    pallas_call x1, Pallas kernels, place(): pl.pallas_call(functools.partial(place_kernel, cut, slots), out_shape=jax...  29.9 us

profile of v4, /device:TPU:9, one launch (start us, length us, event | category | flops | bytes accessed | tf_op | source)
XLA Modules:
  0.0 403.4 jit_solution(4105690441974113460)
XLA Ops:
  0.0 0.7 iota_compare_fusion.1
  0.7 1.3 select_reduce_fusion.owners
  2.1 1.6 broadcast_in_dim.6.gain_ref
  3.7 369.8 %exchange.1 = (bf16[8,896,2048]{2,1,0:T(8,128)(2,1)}, bf16[2,8,896,1024]{3,2,1,0:T(8,128)(2,1)S(1)}) custom-call(s32[8]{0:T(128)} %select_reduce_fusion.owners, f32[896,1]{1,0:T(8,128)} %broadcast_in_dim.6.gain_ref, bf16[4,896,512]{2,1,0:T(8,128)(2,1)} %gate_hbm.1, bf16[4,896,512]{2,1,0:T(8,128)(2,1)} %up_hbm.1), custom_call_target="tpu_custom_call" | custom-call | tf_op jit(solution)/shard_map/exchange/pallas_call | solution.py:262
  373.6 29.9 %place.1 = bf16[7168,4096]{1,0:T(8,128)(2,1)} custom-call(s32[8]{0:T(128)} %matching.1, bf16[8,896,2048]{2,1,0:T(8,128)(2,1)} %get-tuple-element.7.in_ref, bf16[2,8,896,1024]{3,2,1,0:T(8,128)(2,1)S(1)} %get-tuple-element.8.near_ref), custom_call_target="tpu_custom_call" | custom-call | tf_op jit(solution)/shard_map/place/pallas_call | solution.py:355
